TPU v7x, 32 devices: a whole 2x2x4 slice. The times are simulated.
32 devices in a mesh: expert: 8 (over z, core), mp: 4 (over y, x).
Axes of the slice: x: 2, y: 2, z: 4, core: 2. Of those that a mesh axis runs over, the one named last changes fastest.
Arguments:
- tokens: bfloat16 [1024, 4096], P('expert', 'mp'), may hold values from -6 to 6
- expert_ids: int32 [1024, 1], P('expert'), may hold values from 0 to 7; in each aligned block of 128 rows (0 to 127, 128 to 255, ...) at most 32 rows name the same one
- seq_lengths: int32 [8], P('expert'), may hold values from 64 to 128, as said below
- hidden_cotangent: bfloat16 [8, 256, 6144], P('expert', None, 'mp'), may hold values from -6 to 6
- w_in: bfloat16 [8, 4096, 6144], P('expert', None, 'mp'), may hold values from -0.09375 to 0.09375
Outputs:
- grad_tokens: bfloat16 [1024, 4096], P('expert', 'mp')
Inputs may be any that keep to these rules, and one draw needn't show every extreme that they name: `expert_ids`: in each aligned block of 128 rows no expert is named by more than 32 rows, a bound that some block reaches. `seq_lengths`: some sequence is full and some has exactly 64 live positions.
All inputs are finite; a program needn't handle non-finite values.
Results may differ from a plain program's by a relative error of at most 0.014.
Values may be sent and summed in bfloat16 or wider, within the bound.
A program may use at most 64 MiB of HBM per device.

v0:
```python
import functools
import math

import jax
import jax.numpy as jnp
from jax import lax
from jax.experimental import pallas as pl
from jax.experimental.pallas import tpu as pltpu
from jax.sharding import PartitionSpec as P

SEQ_LEN = 128
MESH = pl.DeviceIdType.MESH
ORDER = (0, 1, 4, 5, 2, 3, 6, 7)
RETURN = (3, 1, 2, 0)
TILE = 512
def gelu_slope(preact):
    coeff = math.sqrt(2.0 / math.pi)
    squashed = jnp.tanh(coeff * (preact + 0.044715 * preact * preact * preact))
    return 0.5 * (1.0 + squashed) + 0.5 * preact * (1.0 - squashed * squashed) * coeff * (
        1.0 + 3.0 * 0.044715 * preact * preact
    )


def per_device(tokens, expert_ids, seq_lengths, hidden_cotangent, w_in):
    tok_dev = tokens.shape[0]
    experts = w_in.shape[0] * lax.axis_size("expert")
    capacity = max(2, 2 * tok_dev // experts)
    position = jnp.arange(tok_dev, dtype=jnp.int32)
    seq_index = position // SEQ_LEN
    seq_length = jnp.sum(
        jnp.where(
            seq_index[:, None] == jnp.arange(seq_lengths.shape[0], dtype=jnp.int32)[None, :],
            seq_lengths[None, :],
            0,
        ),
        axis=1,
    )
    live_mask = position % SEQ_LEN < seq_length
    expert_row = expert_ids[:, 0]
    onehot = (
        (expert_row[:, None] == jnp.arange(experts, dtype=jnp.int32)[None, :]) & live_mask[:, None]
    ).astype(jnp.int32)
    slot_rank = jnp.sum(jnp.cumsum(onehot, axis=0) * onehot, axis=1) - 1
    target = jnp.where(live_mask, expert_row * capacity + slot_rank, experts * capacity)
    buffer = (
        jnp.zeros((experts * capacity + 1,) + tokens.shape[1:], tokens.dtype).at[target].set(tokens)
    )
    arrived = lax.all_to_all(
        buffer[:-1].reshape((experts, capacity) + tokens.shape[1:]),
        "expert",
        split_axis=0,
        concat_axis=0,
        tiled=True,
    )
    slot_count = arrived.shape[0] * capacity
    features = lax.all_gather(
        arrived.reshape(slot_count, arrived.shape[2]), "mp", axis=1, tiled=True
    )
    weight = w_in[0]
    pre_act = jnp.dot(features, weight, preferred_element_type=jnp.float32)
    hidden_grad = (hidden_cotangent[0].astype(jnp.float32) * gelu_slope(pre_act)).astype(
        jnp.bfloat16
    )
    partial_value = lax.dot_general(
        hidden_grad, weight, (((1,), (1,)), ((), ())), preferred_element_type=jnp.float32
    ).astype(jnp.bfloat16)
    partial_value = lax.optimization_barrier(partial_value)
    summed = lax.psum_scatter(
        partial_value.astype(jnp.float32).astype(jnp.bfloat16),
        "mp",
        scatter_dimension=1,
        tiled=True,
    )
    returned = lax.all_to_all(
        summed.reshape(arrived.shape[0], capacity, summed.shape[1]),
        "expert",
        split_axis=0,
        concat_axis=0,
        tiled=True,
    )
    flat_rows = returned.reshape((experts * capacity,) + returned.shape[2:])
    padded = jnp.concatenate(
        [flat_rows, jnp.zeros((1,) + flat_rows.shape[1:], flat_rows.dtype)], axis=0
    )
    return padded[target]


def flip(index, difference, bits):
    total = 0
    for bit in range(bits):
        value = lax.rem(index // (1 << bit), 2)
        total = total + (1 << bit) * ((1 - value) if difference >> bit & 1 else value)
    return total


def kernel(
    cap,
    tokens_hbm,
    ids_hbm,
    lengths_ref,
    cot_hbm,
    w_hbm,
    out_ref,
    tokens_ref,
    ids_ref,
    w_v,
    cot_v,
    send_rows,
    feats,
    parts,
    before_act,
    hidden,
    combine,
    diag_in,
    direct_in,
    sum_in,
    sum_out,
    done_rows,
    back_rows,
    local_sem,
    send_sem,
    recv_sem,
):
    expert, place = lax.axis_index("expert"), lax.axis_index("mp")
    peers = [flip(expert, k, 3) for k in ORDER]
    side = [None, (expert, flip(place, 1, 2)), (expert, flip(place, 2, 2))]
    tok, width = tokens_ref.shape
    ff = w_v.shape[2]
    half = cap // 2
    first, second = pl.ds(0, half), pl.ds(half, half)

    barrier = pltpu.get_barrier_semaphore()
    greeted = [(peer, place) for peer in peers[1:]] + side[1:]
    for device in greeted:
        pl.semaphore_signal(barrier, inc=1, device_id=device, device_id_type=MESH)

    inputs = [
        pltpu.make_async_copy(source, target, local_sem.at[12 + n])
        for n, (source, target) in enumerate(
            ((ids_hbm, ids_ref), (tokens_hbm, tokens_ref))
        )
    ]
    for load in inputs:
        load.start()
    loads = []
    for j in range(4):
        start = pl.multiple_of(flip(place, j, 2) * width, width)
        loads.append(
            pltpu.make_async_copy(w_hbm.at[0, pl.ds(start, width)], w_v.at[j], local_sem.at[j])
        )
    cot_loads = []
    for p in range(8):
        start = pl.multiple_of(peers[p] * cap, cap)
        cot_loads.append(
            pltpu.make_async_copy(
                cot_hbm.at[0, pl.ds(start, cap)], cot_v.at[p], local_sem.at[4 + p]
            )
        )

    position = lax.broadcasted_iota(jnp.int32, (1, tok), 1)
    limit = jnp.zeros((1, tok), jnp.int32)
    inputs[0].wait()
    for i in range(lengths_ref.shape[0]):
        limit = jnp.where(position // SEQ_LEN == i, lengths_ref[i], limit)
    live = position % SEQ_LEN < limit
    away = jnp.bitwise_xor(ids_ref[...], expert)
    rank_of = jnp.zeros((1, tok), jnp.int32)
    for p, k in enumerate(ORDER):
        rank_of = jnp.where(away == k, p, rank_of)
    rank_of = jnp.where(live, rank_of, -1)
    onehot = jnp.where(
        lax.broadcasted_iota(jnp.int32, (16, tok), 0) == rank_of, 1.0, 0.0
    )
    before = lax.broadcasted_iota(jnp.int32, (tok, tok), 0) <= lax.broadcasted_iota(
        jnp.int32, (tok, tok), 1
    )
    counts = jnp.dot(
        onehot.astype(jnp.bfloat16),
        jnp.where(before, 1.0, 0.0).astype(jnp.bfloat16),
        preferred_element_type=jnp.float32,
    )
    slot = jnp.sum(counts * onehot, axis=0, keepdims=True) - 1.0
    slot = jnp.where(live, slot + (rank_of * cap).astype(jnp.float32), -1.0)
    slots = lax.broadcasted_iota(jnp.int32, (8 * cap, tok), 0).astype(jnp.float32)
    chosen = jnp.where(slots == slot, 1.0, 0.0)
    inputs[1].wait()
    placed = jnp.dot(
        chosen.astype(jnp.bfloat16), tokens_ref[...], preferred_element_type=jnp.float32
    ).astype(jnp.bfloat16)
    feats[0, 0] = placed[:cap]
    for p in range(1, 8):
        send_rows[p] = placed[p * cap : (p + 1) * cap]

    pl.semaphore_wait(barrier, len(greeted))

    started = []
    numbers = iter(range(1000))

    def remote(source, target, device):
        n = next(numbers)
        return pltpu.make_async_remote_copy(
            src_ref=source,
            dst_ref=target,
            send_sem=send_sem.at[n],
            recv_sem=recv_sem.at[n],
            device_id=device,
            device_id_type=MESH,
        )

    def go(copy):
        copy.start()
        started.append(copy)

    out_copies = [None] + [
        remote(send_rows.at[p], feats.at[0, p], (peers[p], place)) for p in range(1, 8)
    ]
    back_copies = [None] + [
        remote(done_rows.at[p], back_rows.at[p], (peers[p], place)) for p in range(1, 8)
    ]
    pairs = [pl.ds(2 * q, 2) for q in range(4)]
    gather = [
        [None] + [remote(feats.at[0, pair], feats.at[d, pair], side[d]) for d in (1, 2)]
        for pair in pairs
    ]
    relay = [
        [
            None,
            remote(feats.at[2, pair, second], feats.at[3, pair, second], side[1]),
            remote(feats.at[1, pair, first], feats.at[3, pair, first], side[2]),
        ]
        for pair in pairs
    ]
    rows = [None, first, second]
    diag = [
        [None]
        + [remote(parts.at[3, pair, rows[d]], diag_in.at[d - 1, pair], side[d]) for d in (1, 2)]
        for pair in pairs
    ]
    direct = [
        [None]
        + [remote(parts.at[d, pair, rows[d]], direct_in.at[d - 1, pair], side[d]) for d in (1, 2)]
        for pair in pairs
    ]
    summed = [
        [None]
        + [remote(sum_out.at[d - 1, pair], sum_in.at[d - 1, pair], side[d]) for d in (1, 2)]
        for pair in pairs
    ]

    for p in range(1, 8):
        go(out_copies[p])
    for load in loads + cot_loads:
        load.start()

    def gather_start(q):
        for p in (2 * q, 2 * q + 1):
            if p:
                out_copies[p].wait_recv()
        go(gather[q][1])
        go(gather[q][2])

    def gather_relay(q):
        gather[q][1].wait_recv()
        go(relay[q][2])
        gather[q][2].wait_recv()
        go(relay[q][1])

    def gather_end(q):
        relay[q][1].wait_recv()
        relay[q][2].wait_recv()

    rows_all = 8 * cap

    def hidden_tile(first_block, last_block, n):
        columns = slice(n * TILE, (n + 1) * TILE)
        total = None if first_block == 0 else before_act[:, columns]
        for j in range(first_block, last_block):
            product = jnp.dot(
                feats[j].reshape(rows_all, width),
                w_v[j, :, columns],
                preferred_element_type=jnp.float32,
            )
            total = product if total is None else total + product
        if last_block < 4:
            before_act[:, columns] = total
        else:
            cotangent = cot_v[:, :, columns].reshape(rows_all, TILE).astype(jnp.float32)
            hidden[:, columns] = (cotangent * gelu_slope(total)).astype(jnp.bfloat16)

    def part_block(j):
        for n in range(width // TILE):
            columns = slice(n * TILE, (n + 1) * TILE)
            block = lax.dot_general(
                hidden[...],
                w_v[j, columns, :],
                (((1,), (1,)), ((), ())),
                preferred_element_type=jnp.float32,
            )
            parts[j, :, :, columns] = block.astype(jnp.bfloat16).reshape(8, cap, TILE)

    def sum_step(q, d):
        pair, other = pairs[q], 3 - d
        diag[q][d].wait_recv()
        sum_out[other - 1, pair] = (
            parts[other, pair, rows[d]].astype(jnp.float32)
            + diag_in[d - 1, pair].astype(jnp.float32)
        ).astype(jnp.bfloat16)
        go(summed[q][other])

    def final_step(q):
        pair = pairs[q]
        for d in (1, 2):
            direct[q][d].wait_recv()
            summed[q][3 - d].wait_recv()
            total = (
                parts[0, pair, rows[d]].astype(jnp.float32)
                + direct_in[d - 1, pair].astype(jnp.float32)
                + sum_in[2 - d, pair].astype(jnp.float32)
            ).astype(jnp.bfloat16)
            done_rows[pair, rows[d]] = total
        for p in (2 * q, 2 * q + 1):
            if p:
                go(back_copies[p])
            else:
                back_rows[0] = done_rows[0]

    tiles = ff // TILE
    gather_start(0)
    combine[...] = chosen.T.astype(jnp.bfloat16)
    gather_start(1)
    gather_relay(0)
    gather_start(2)
    gather_relay(1)
    gather_start(3)
    for load in loads + cot_loads:
        load.wait()
    hidden_tile(0, 1, 0)
    gather_relay(2)
    for n in range(1, tiles):
        hidden_tile(0, 1, n)
    gather_relay(3)
    for n in range(tiles):
        hidden_tile(1, 3, n)
    for q in range(4):
        gather_end(q)
    for n in range(tiles):
        hidden_tile(3, 4, n)
    part_block(3)
    for q in RETURN:
        go(diag[q][1])
        go(diag[q][2])
    part_block(1)
    for q in RETURN:
        sum_step(q, 2)
    part_block(2)
    for q in RETURN:
        sum_step(q, 1)
    for q in RETURN:
        go(direct[q][1])
        go(direct[q][2])
    part_block(0)
    for q in RETURN:
        final_step(q)
    for p in range(1, 8):
        back_copies[p].wait_recv()
    out_ref[...] = jnp.dot(
        combine[...],
        back_rows[...].reshape(8 * cap, width),
        preferred_element_type=jnp.float32,
    ).astype(out_ref.dtype)
    for copy in started:
        copy.wait_send()


def one_kernel(tokens, expert_ids, seq_lengths, hidden_cotangent, w_in):
    tok, width = tokens.shape
    ff = w_in.shape[2]
    cap = hidden_cotangent.shape[1] // 8
    half = cap // 2
    bf16 = jnp.bfloat16
    copies = 7 + 7 + 4 * 10
    vmem, anywhere = pl.BlockSpec(memory_space=pltpu.VMEM), pl.BlockSpec(memory_space=pl.ANY)
    smem = pl.BlockSpec(memory_space=pltpu.SMEM)
    return pl.pallas_call(
        functools.partial(kernel, cap),
        out_shape=jax.ShapeDtypeStruct((tok, width), tokens.dtype),
        in_specs=[anywhere, anywhere, smem, anywhere, anywhere],
        out_specs=vmem,
        scratch_shapes=[
            pltpu.VMEM((tok, width), bf16),
            pltpu.VMEM((1, tok), jnp.int32),
            pltpu.VMEM((4, width, ff), bf16),
            pltpu.VMEM((8, cap, ff), bf16),
            pltpu.VMEM((8, cap, width), bf16),
            pltpu.VMEM((4, 8, cap, width), bf16),
            pltpu.VMEM((4, 8, cap, width), bf16),
            pltpu.VMEM((8 * cap, ff), jnp.float32),
            pltpu.VMEM((8 * cap, ff), bf16),
            pltpu.VMEM((tok, 8 * cap), bf16),
            pltpu.VMEM((2, 8, half, width), bf16),
            pltpu.VMEM((2, 8, half, width), bf16),
            pltpu.VMEM((2, 8, half, width), bf16),
            pltpu.VMEM((2, 8, half, width), bf16),
            pltpu.VMEM((8, cap, width), bf16),
            pltpu.VMEM((8, cap, width), bf16),
            pltpu.SemaphoreType.DMA((14,)),
            pltpu.SemaphoreType.DMA((copies,)),
            pltpu.SemaphoreType.DMA((copies,)),
        ],
        compiler_params=pltpu.CompilerParams(
            collective_id=0, has_side_effects=True, vmem_limit_bytes=58 << 20
        ),
        cost_estimate=pl.CostEstimate(
            flops=4 * 8 * cap * 4 * width * ff,
            bytes_accessed=2 * 4 * width * ff,
            transcendentals=8 * cap * ff,
        ),
    )(tokens, expert_ids.reshape(1, tok), seq_lengths, hidden_cotangent, w_in)


def solution(mesh):
    in_specs = (
        P("expert", "mp"),
        P("expert", None),
        P("expert"),
        P("expert", None, "mp"),
        P("expert", None, "mp"),
    )
    out_specs = P("expert", "mp")
    small = mesh.shape["mp"] == 4 and mesh.shape["expert"] == 8
    return jax.shard_map(
        one_kernel if small else per_device,
        mesh=mesh,
        in_specs=in_specs,
        out_specs=out_specs,
        check_vma=False,
    )
```

profile of v0, /device:TPU:1, one launch (start us, length us, event | category | flops | bytes accessed | tf_op | source)
XLA Modules:
  0.0 62.7 jit_solution(16051497006357303387)
XLA Ops:
  0.7 60.3 %shard_map.55 = bf16[128,1024]{1,0:T(8,128)(2,1)} custom-call(bf16[128,1024]{1,0:T(8,128)(2,1)} %tokens_hbm.1, s32[1,128]{1,0:T(1,128)} %bitcast.1, s32[1]{0:T(128)S(6)} %copy.7.lengths_ref, bf16[1,256,1536]{2,1,0:T(8,128)(2,1)} %cot_hbm.1, bf16[1,4096,1536]{2,1,0:T(8,128)(2,1)} %w_hbm.1), custom_call_target="tpu_custom_call" | custom-call | flops 6442450944 | bytes 12582912 | tf_op jit(solution)/shard_map/pallas_call | solution.py:384
  61.0 1.7 %copy.8 = bf16[128,1024]{1,0:T(8,128)(2,1)} copy(bf16[128,1024]{1,0:T(8,128)(2,1)} %shard_map.55) | data formatting | bytes 524288
where the time goes:
time: 62.8 us; the launch traced here: 62.7 us
  Pallas kernels  60.3 us (96%)
  local copies, waits for them, and re-layouts  1.67 us (3%)
  between operations  0.66 us (1%)
    pallas_call x1, Pallas kernels, one_kernel(): pl.pallas_call(functools.partial(kernel, cap), out_shape=jax.ShapeDtypeSt...  60.3 us
    unnamed x1, local copies, waits for them, and re-layouts  1.67 us

commit v1 on v0

--- a/solution.py
+++ b/solution.py
@@ -10,8 +10,7 @@
 
 SEQ_LEN = 128
 MESH = pl.DeviceIdType.MESH
-ORDER = (0, 1, 4, 5, 2, 3, 6, 7)
-RETURN = (3, 1, 2, 0)
+ORDER = (0, 1, 4, 5, 6, 7, 2, 3)
 TILE = 512
 def gelu_slope(preact):
     coeff = math.sqrt(2.0 / math.pi)
@@ -108,7 +107,6 @@
     send_rows,
     feats,
     parts,
-    before_act,
     hidden,
     combine,
     diag_in,
@@ -220,8 +218,9 @@
     pairs = [pl.ds(2 * q, 2) for q in range(4)]
     gather = [
         [None] + [remote(feats.at[0, pair], feats.at[d, pair], side[d]) for d in (1, 2)]
-        for pair in pairs
-    ]
+        for pair in pairs[1:]
+    ]
+    gather = [None] + gather
     relay = [
         [
             None,
@@ -247,47 +246,56 @@
         for pair in pairs
     ]
 
+    own = [None] + [remote(feats.at[0, 0], feats.at[d, 0], side[d]) for d in (1, 2)]
+    peer = [None] + [remote(feats.at[0, 1], feats.at[d, 1], side[d]) for d in (1, 2)]
+    go(own[1])
+    go(own[2])
     for p in range(1, 8):
         go(out_copies[p])
     for load in loads + cot_loads:
         load.start()
 
     def gather_start(q):
-        for p in (2 * q, 2 * q + 1):
-            if p:
-                out_copies[p].wait_recv()
+        if q == 0:
+            out_copies[1].wait_recv()
+            go(peer[1])
+            go(peer[2])
+            return
+        out_copies[2 * q].wait_recv()
+        out_copies[2 * q + 1].wait_recv()
         go(gather[q][1])
         go(gather[q][2])
 
     def gather_relay(q):
-        gather[q][1].wait_recv()
-        go(relay[q][2])
-        gather[q][2].wait_recv()
-        go(relay[q][1])
+        for d in (1, 2):
+            if q == 0:
+                own[d].wait_recv()
+                peer[d].wait_recv()
+            else:
+                gather[q][d].wait_recv()
+            go(relay[q][3 - d])
 
     def gather_end(q):
         relay[q][1].wait_recv()
         relay[q][2].wait_recv()
 
-    rows_all = 8 * cap
-
-    def hidden_tile(first_block, last_block, n):
-        columns = slice(n * TILE, (n + 1) * TILE)
-        total = None if first_block == 0 else before_act[:, columns]
-        for j in range(first_block, last_block):
+    rows_all = 4 * cap
+
+    def hidden_tile(g, n):
+        group, columns = slice(4 * g, 4 * g + 4), slice(n * TILE, (n + 1) * TILE)
+        total = None
+        for j in range(4):
             product = jnp.dot(
-                feats[j].reshape(rows_all, width),
+                feats[j, group].reshape(rows_all, width),
                 w_v[j, :, columns],
                 preferred_element_type=jnp.float32,
             )
             total = product if total is None else total + product
-        if last_block < 4:
-            before_act[:, columns] = total
-        else:
-            cotangent = cot_v[:, :, columns].reshape(rows_all, TILE).astype(jnp.float32)
-            hidden[:, columns] = (cotangent * gelu_slope(total)).astype(jnp.bfloat16)
-
-    def part_block(j):
+        cotangent = cot_v[group, :, columns].reshape(rows_all, TILE).astype(jnp.float32)
+        hidden[:, columns] = (cotangent * gelu_slope(total)).astype(jnp.bfloat16)
+
+    def part_block(g, j):
+        group = slice(4 * g, 4 * g + 4)
         for n in range(width // TILE):
             columns = slice(n * TILE, (n + 1) * TILE)
             block = lax.dot_general(
@@ -296,7 +304,7 @@
                 (((1,), (1,)), ((), ())),
                 preferred_element_type=jnp.float32,
             )
-            parts[j, :, :, columns] = block.astype(jnp.bfloat16).reshape(8, cap, TILE)
+            parts[j, group, :, columns] = block.astype(jnp.bfloat16).reshape(4, cap, TILE)
 
     def sum_step(q, d):
         pair, other = pairs[q], 3 - d
@@ -327,40 +335,57 @@
     tiles = ff // TILE
     gather_start(0)
     combine[...] = chosen.T.astype(jnp.bfloat16)
+    gather_relay(0)
     gather_start(1)
-    gather_relay(0)
-    gather_start(2)
     gather_relay(1)
-    gather_start(3)
     for load in loads + cot_loads:
         load.wait()
-    hidden_tile(0, 1, 0)
-    gather_relay(2)
+    gather_end(0)
+    gather_end(1)
+    hidden_tile(0, 0)
+    gather_start(2)
     for n in range(1, tiles):
-        hidden_tile(0, 1, n)
-    gather_relay(3)
-    for n in range(tiles):
-        hidden_tile(1, 3, n)
-    for q in range(4):
-        gather_end(q)
-    for n in range(tiles):
-        hidden_tile(3, 4, n)
-    part_block(3)
-    for q in RETURN:
+        hidden_tile(0, n)
+    gather_start(3)
+    part_block(0, 3)
+    for q in (0, 1):
         go(diag[q][1])
         go(diag[q][2])
-    part_block(1)
-    for q in RETURN:
-        sum_step(q, 2)
-    part_block(2)
-    for q in RETURN:
-        sum_step(q, 1)
-    for q in RETURN:
+    gather_relay(2)
+    part_block(0, 1)
+    sum_step(0, 2)
+    gather_relay(3)
+    sum_step(1, 2)
+    part_block(0, 2)
+    sum_step(0, 1)
+    sum_step(1, 1)
+    for q in (0, 1):
         go(direct[q][1])
         go(direct[q][2])
-    part_block(0)
-    for q in RETURN:
-        final_step(q)
+    part_block(0, 0)
+    gather_end(2)
+    gather_end(3)
+    hidden_tile(1, 0)
+    for n in range(1, tiles):
+        hidden_tile(1, n)
+    part_block(1, 3)
+    for q in (2, 3):
+        go(diag[q][1])
+        go(diag[q][2])
+    final_step(1)
+    part_block(1, 1)
+    sum_step(2, 2)
+    sum_step(3, 2)
+    part_block(1, 2)
+    sum_step(2, 1)
+    sum_step(3, 1)
+    for q in (2, 3):
+        go(direct[q][1])
+        go(direct[q][2])
+    final_step(0)
+    part_block(1, 0)
+    final_step(2)
+    final_step(3)
     for p in range(1, 8):
         back_copies[p].wait_recv()
     out_ref[...] = jnp.dot(
@@ -378,7 +403,7 @@
     cap = hidden_cotangent.shape[1] // 8
     half = cap // 2
     bf16 = jnp.bfloat16
-    copies = 7 + 7 + 4 * 10
+    copies = 7 + 7 + 4 * 10 + 2
     vmem, anywhere = pl.BlockSpec(memory_space=pltpu.VMEM), pl.BlockSpec(memory_space=pl.ANY)
     smem = pl.BlockSpec(memory_space=pltpu.SMEM)
     return pl.pallas_call(
@@ -394,8 +419,7 @@
             pltpu.VMEM((8, cap, width), bf16),
             pltpu.VMEM((4, 8, cap, width), bf16),
             pltpu.VMEM((4, 8, cap, width), bf16),
-            pltpu.VMEM((8 * cap, ff), jnp.float32),
-            pltpu.VMEM((8 * cap, ff), bf16),
+            pltpu.VMEM((4 * cap, ff), bf16),
             pltpu.VMEM((tok, 8 * cap), bf16),
             pltpu.VMEM((2, 8, half, width), bf16),
             pltpu.VMEM((2, 8, half, width), bf16),

time: 62.8 us -> 62.2 us (level)
  no operation moved by 1% of the time
where the time goes in v1:
time: 62.2 us; the launch traced here: 62.1 us
  Pallas kernels  59.8 us (96%)
  local copies, waits for them, and re-layouts  1.67 us (3%)
  between operations  0.66 us (1%)
    pallas_call x1, Pallas kernels, one_kernel(): pl.pallas_call(functools.partial(kernel, cap), out_shape=jax.ShapeDtypeSt...  59.8 us
    unnamed x1, local copies, waits for them, and re-layouts  1.67 us

profile of v1, /device:TPU:1, one launch (start us, length us, event | category | flops | bytes accessed | tf_op | source)
XLA Modules:
  0.0 62.1 jit_solution(2532463787266377681)
XLA Ops:
  0.7 59.8 %shard_map.55 = bf16[128,1024]{1,0:T(8,128)(2,1)} custom-call(bf16[128,1024]{1,0:T(8,128)(2,1)} %tokens_hbm.1, s32[1,128]{1,0:T(1,128)} %bitcast.1, s32[1]{0:T(128)S(6)} %copy.7.lengths_ref, bf16[1,256,1536]{2,1,0:T(8,128)(2,1)} %cot_hbm.1, bf16[1,4096,1536]{2,1,0:T(8,128)(2,1)} %w_hbm.1), custom_call_target="tpu_custom_call" | custom-call | flops 6442450944 | bytes 12582912 | tf_op jit(solution)/shard_map/pallas_call | solution.py:409
  60.4 1.7 %copy.8 = bf16[128,1024]{1,0:T(8,128)(2,1)} copy(bf16[128,1024]{1,0:T(8,128)(2,1)} %shard_map.55) | data formatting | bytes 524288

commit v2 on v0

--- a/solution.py
+++ b/solution.py
@@ -220,8 +220,9 @@
     pairs = [pl.ds(2 * q, 2) for q in range(4)]
     gather = [
         [None] + [remote(feats.at[0, pair], feats.at[d, pair], side[d]) for d in (1, 2)]
-        for pair in pairs
-    ]
+        for pair in pairs[1:]
+    ]
+    gather = [None] + gather
     relay = [
         [
             None,
@@ -247,23 +248,34 @@
         for pair in pairs
     ]
 
-    for p in range(1, 8):
+    own = [None] + [remote(feats.at[0, 0], feats.at[d, 0], side[d]) for d in (1, 2)]
+    peer = [None] + [remote(feats.at[0, 1], feats.at[d, 1], side[d]) for d in (1, 2)]
+    go(own[1])
+    go(own[2])
+    for p in (1, 2, 3):
         go(out_copies[p])
     for load in loads + cot_loads:
         load.start()
 
     def gather_start(q):
-        for p in (2 * q, 2 * q + 1):
-            if p:
-                out_copies[p].wait_recv()
+        if q == 0:
+            out_copies[1].wait_recv()
+            go(peer[1])
+            go(peer[2])
+            return
+        out_copies[2 * q].wait_recv()
+        out_copies[2 * q + 1].wait_recv()
         go(gather[q][1])
         go(gather[q][2])
 
     def gather_relay(q):
-        gather[q][1].wait_recv()
-        go(relay[q][2])
-        gather[q][2].wait_recv()
-        go(relay[q][1])
+        for d in (1, 2):
+            if q == 0:
+                own[d].wait_recv()
+                peer[d].wait_recv()
+            else:
+                gather[q][d].wait_recv()
+            go(relay[q][3 - d])
 
     def gather_end(q):
         relay[q][1].wait_recv()
@@ -291,12 +303,12 @@
         for n in range(width // TILE):
             columns = slice(n * TILE, (n + 1) * TILE)
             block = lax.dot_general(
+                w_v[j, columns, :],
                 hidden[...],
-                w_v[j, columns, :],
                 (((1,), (1,)), ((), ())),
                 preferred_element_type=jnp.float32,
             )
-            parts[j, :, :, columns] = block.astype(jnp.bfloat16).reshape(8, cap, TILE)
+            parts[j, :, :, columns] = block.T.astype(jnp.bfloat16).reshape(8, cap, TILE)
 
     def sum_step(q, d):
         pair, other = pairs[q], 3 - d
@@ -327,16 +339,17 @@
     tiles = ff // TILE
     gather_start(0)
     combine[...] = chosen.T.astype(jnp.bfloat16)
+    gather_relay(0)
     gather_start(1)
-    gather_relay(0)
+    for p in (6, 7, 4, 5):
+        go(out_copies[p])
+    gather_relay(1)
     gather_start(2)
-    gather_relay(1)
+    gather_relay(2)
     gather_start(3)
     for load in loads + cot_loads:
         load.wait()
-    hidden_tile(0, 1, 0)
-    gather_relay(2)
-    for n in range(1, tiles):
+    for n in range(tiles):
         hidden_tile(0, 1, n)
     gather_relay(3)
     for n in range(tiles):
@@ -349,16 +362,13 @@
     for q in RETURN:
         go(diag[q][1])
         go(diag[q][2])
-    part_block(1)
+    for j in (1, 2, 0):
+        part_block(j)
     for q in RETURN:
         sum_step(q, 2)
-    part_block(2)
-    for q in RETURN:
         sum_step(q, 1)
-    for q in RETURN:
         go(direct[q][1])
         go(direct[q][2])
-    part_block(0)
     for q in RETURN:
         final_step(q)
     for p in range(1, 8):
@@ -378,7 +388,7 @@
     cap = hidden_cotangent.shape[1] // 8
     half = cap // 2
     bf16 = jnp.bfloat16
-    copies = 7 + 7 + 4 * 10
+    copies = 7 + 7 + 4 * 10 + 2
     vmem, anywhere = pl.BlockSpec(memory_space=pltpu.VMEM), pl.BlockSpec(memory_space=pl.ANY)
     smem = pl.BlockSpec(memory_space=pltpu.SMEM)
     return pl.pallas_call(

time: 62.8 us -> 61.1 us (0.973)
  Pallas kernels: 60.3 us -> 58.6 us
    pallas_call x1, Pallas kernels: 60.3 us -> 58.6 us  [one_kernel(): pl.pallas_call(functools.partial(kernel, cap), out_shape=jax.ShapeDtypeSt...]
where the time goes in v2:
time: 61.1 us; the launch traced here: 60.9 us
  Pallas kernels  58.6 us (96%)
  local copies, waits for them, and re-layouts  1.67 us (3%)
  between operations  0.66 us (1%)
    pallas_call x1, Pallas kernels, one_kernel(): pl.pallas_call(functools.partial(kernel, cap), out_shape=jax.ShapeDtypeSt...  58.6 us
    unnamed x1, local copies, waits for them, and re-layouts  1.67 us

profile of v2, /device:TPU:1, one launch (start us, length us, event | category | flops | bytes accessed | tf_op | source)
XLA Modules:
  0.0 60.9 jit_solution(8074872080750018102)
XLA Ops:
  0.7 58.6 %shard_map.55 = bf16[128,1024]{1,0:T(8,128)(2,1)} custom-call(bf16[128,1024]{1,0:T(8,128)(2,1)} %tokens_hbm.1, s32[1,128]{1,0:T(1,128)} %bitcast.1, s32[1]{0:T(128)S(6)} %copy.7.lengths_ref, bf16[1,256,1536]{2,1,0:T(8,128)(2,1)} %cot_hbm.1, bf16[1,4096,1536]{2,1,0:T(8,128)(2,1)} %w_hbm.1), custom_call_target="tpu_custom_call" | custom-call | flops 6442450944 | bytes 12582912 | tf_op jit(solution)/shard_map/pallas_call | solution.py:394
  59.2 1.7 %copy.8 = bf16[128,1024]{1,0:T(8,128)(2,1)} copy(bf16[128,1024]{1,0:T(8,128)(2,1)} %shard_map.55) | data formatting | bytes 524288

commit v3 on v1

--- a/solution.py
+++ b/solution.py
@@ -10,7 +10,8 @@
 
 SEQ_LEN = 128
 MESH = pl.DeviceIdType.MESH
-ORDER = (0, 1, 4, 5, 6, 7, 2, 3)
+ORDER = (0, 1, 4, 5, 2, 3, 6, 7)
+RETURN = (3, 2, 1, 0)
 TILE = 512
 def gelu_slope(preact):
     coeff = math.sqrt(2.0 / math.pi)
@@ -250,9 +251,9 @@
     peer = [None] + [remote(feats.at[0, 1], feats.at[d, 1], side[d]) for d in (1, 2)]
     go(own[1])
     go(own[2])
-    for p in range(1, 8):
+    for p in (1, 2, 3):
         go(out_copies[p])
-    for load in loads + cot_loads:
+    for load in cot_loads:
         load.start()
 
     def gather_start(q):
@@ -299,12 +300,12 @@
         for n in range(width // TILE):
             columns = slice(n * TILE, (n + 1) * TILE)
             block = lax.dot_general(
+                w_v[j, columns, :],
                 hidden[...],
-                w_v[j, columns, :],
                 (((1,), (1,)), ((), ())),
                 preferred_element_type=jnp.float32,
             )
-            parts[j, group, :, columns] = block.astype(jnp.bfloat16).reshape(4, cap, TILE)
+            parts[j, group, :, columns] = block.T.astype(jnp.bfloat16).reshape(4, cap, TILE)
 
     def sum_step(q, d):
         pair, other = pairs[q], 3 - d
@@ -334,58 +335,58 @@
 
     tiles = ff // TILE
     gather_start(0)
+    loads[0].start()
     combine[...] = chosen.T.astype(jnp.bfloat16)
     gather_relay(0)
+    loads[1].start()
     gather_start(1)
+    for p in (6, 7, 4, 5):
+        go(out_copies[p])
+    loads[2].start()
     gather_relay(1)
+    loads[3].start()
+    gather_start(2)
     for load in loads + cot_loads:
         load.wait()
     gather_end(0)
     gather_end(1)
     hidden_tile(0, 0)
-    gather_start(2)
+    gather_relay(2)
+    gather_start(3)
     for n in range(1, tiles):
         hidden_tile(0, n)
-    gather_start(3)
+    gather_relay(3)
     part_block(0, 3)
-    for q in (0, 1):
+    for q in RETURN[2:]:
         go(diag[q][1])
         go(diag[q][2])
-    gather_relay(2)
-    part_block(0, 1)
-    sum_step(0, 2)
-    gather_relay(3)
-    sum_step(1, 2)
-    part_block(0, 2)
-    sum_step(0, 1)
-    sum_step(1, 1)
-    for q in (0, 1):
+    for j in (1, 2, 0):
+        part_block(0, j)
+    for q in RETURN[2:]:
+        sum_step(q, 2)
+        sum_step(q, 1)
         go(direct[q][1])
         go(direct[q][2])
-    part_block(0, 0)
     gather_end(2)
     gather_end(3)
-    hidden_tile(1, 0)
-    for n in range(1, tiles):
+    for n in range(tiles):
         hidden_tile(1, n)
     part_block(1, 3)
-    for q in (2, 3):
+    for q in RETURN[:2]:
         go(diag[q][1])
         go(diag[q][2])
-    final_step(1)
-    part_block(1, 1)
-    sum_step(2, 2)
-    sum_step(3, 2)
-    part_block(1, 2)
-    sum_step(2, 1)
-    sum_step(3, 1)
-    for q in (2, 3):
+    final_step(RETURN[2])
+    for j in (1, 2):
+        part_block(1, j)
+    for q in RETURN[:2]:
+        sum_step(q, 2)
+        sum_step(q, 1)
         go(direct[q][1])
         go(direct[q][2])
-    final_step(0)
+    final_step(RETURN[3])
     part_block(1, 0)
-    final_step(2)
-    final_step(3)
+    for q in RETURN[:2]:
+        final_step(q)
     for p in range(1, 8):
         back_copies[p].wait_recv()
     out_ref[...] = jnp.dot(

time: 62.2 us -> 59.3 us (0.953)
  Pallas kernels: 59.8 us -> 56.8 us
    pallas_call x1, Pallas kernels: 59.8 us -> 56.8 us  [one_kernel(): pl.pallas_call(functools.partial(kernel, cap), out_shape=jax.ShapeDtypeSt...]
where the time goes in v3:
time: 59.3 us; the launch traced here: 59.1 us
  Pallas kernels  56.8 us (96%)
  local copies, waits for them, and re-layouts  1.67 us (3%)
  between operations  0.66 us (1%)
    pallas_call x1, Pallas kernels, one_kernel(): pl.pallas_call(functools.partial(kernel, cap), out_shape=jax.ShapeDtypeSt...  56.8 us
    unnamed x1, local copies, waits for them, and re-layouts  1.67 us

profile of v3, /device:TPU:1, one launch (start us, length us, event | category | flops | bytes accessed | tf_op | source)
XLA Modules:
  0.0 59.1 jit_solution(12261378964358237434)
XLA Ops:
  0.7 56.8 %shard_map.55 = bf16[128,1024]{1,0:T(8,128)(2,1)} custom-call(bf16[128,1024]{1,0:T(8,128)(2,1)} %tokens_hbm.1, s32[1,128]{1,0:T(1,128)} %bitcast.1, s32[1]{0:T(128)S(6)} %copy.7.lengths_ref, bf16[1,256,1536]{2,1,0:T(8,128)(2,1)} %cot_hbm.1, bf16[1,4096,1536]{2,1,0:T(8,128)(2,1)} %w_hbm.1), custom_call_target="tpu_custom_call" | custom-call | flops 6442450944 | bytes 12582912 | tf_op jit(solution)/shard_map/pallas_call | solution.py:410
  57.5 1.7 %copy.8 = bf16[128,1024]{1,0:T(8,128)(2,1)} copy(bf16[128,1024]{1,0:T(8,128)(2,1)} %shard_map.55) | data formatting | bytes 524288

commit v4 on v3

--- a/solution.py
+++ b/solution.py
@@ -353,23 +353,26 @@
     hidden_tile(0, 0)
     gather_relay(2)
     gather_start(3)
-    for n in range(1, tiles):
+    for n in range(1, tiles - 1):
         hidden_tile(0, n)
     gather_relay(3)
+    hidden_tile(0, tiles - 1)
     part_block(0, 3)
     for q in RETURN[2:]:
         go(diag[q][1])
         go(diag[q][2])
-    for j in (1, 2, 0):
+    for j in (1, 2):
         part_block(0, j)
+        for q in RETURN[2:]:
+            go(direct[q][j])
+    part_block(0, 0)
+    gather_end(2)
+    gather_end(3)
+    hidden_tile(1, 0)
     for q in RETURN[2:]:
         sum_step(q, 2)
         sum_step(q, 1)
-        go(direct[q][1])
-        go(direct[q][2])
-    gather_end(2)
-    gather_end(3)
-    for n in range(tiles):
+    for n in range(1, tiles):
         hidden_tile(1, n)
     part_block(1, 3)
     for q in RETURN[:2]:

time: 59.3 us -> 59.8 us (level)
  no operation moved by 1% of the time
where the time goes in v4:
time: 59.8 us; the launch traced here: 59.6 us
  Pallas kernels  57.3 us (96%)
  local copies, waits for them, and re-layouts  1.67 us (3%)
  between operations  0.66 us (1%)
    pallas_call x1, Pallas kernels, one_kernel(): pl.pallas_call(functools.partial(kernel, cap), out_shape=jax.ShapeDtypeSt...  57.3 us
    unnamed x1, local copies, waits for them, and re-layouts  1.67 us

profile of v4, /device:TPU:1, one launch (start us, length us, event | category | flops | bytes accessed | tf_op | source)
XLA Modules:
  0.0 59.6 jit_solution(17046217180178679871)
XLA Ops:
  0.7 57.3 %shard_map.55 = bf16[128,1024]{1,0:T(8,128)(2,1)} custom-call(bf16[128,1024]{1,0:T(8,128)(2,1)} %tokens_hbm.1, s32[1,128]{1,0:T(1,128)} %bitcast.1, s32[1]{0:T(128)S(6)} %copy.7.lengths_ref, bf16[1,256,1536]{2,1,0:T(8,128)(2,1)} %cot_hbm.1, bf16[1,4096,1536]{2,1,0:T(8,128)(2,1)} %w_hbm.1), custom_call_target="tpu_custom_call" | custom-call | flops 6442450944 | bytes 12582912 | tf_op jit(solution)/shard_map/pallas_call | solution.py:413
  57.9 1.7 %copy.8 = bf16[128,1024]{1,0:T(8,128)(2,1)} copy(bf16[128,1024]{1,0:T(8,128)(2,1)} %shard_map.55) | data formatting | bytes 524288
